TPU v7x, 32 devices: a whole 2x2x4 slice. The times are simulated.
32 devices in a mesh: seq: 8 (over y, x, core), ch: 4 (over z).
Axes of the slice: x: 2, y: 2, z: 4, core: 2. Of those that a mesh axis runs over, the one named last changes fastest.
Arguments:
- token_ids: int32 [8192], P('seq'), may hold values from 0 to 511
- embedding: bfloat16 [4096, 512], P('ch'), may hold values from -26 to 26
- projected: bfloat16 [3, 4096, 512], P(None, 'ch'), may hold values from -6 to 6
- short_taps: float32 [7, 3, 4096], P(None, None, 'ch'), may hold values from -2 to 2
- long_filter: bfloat16 [4096, 8192], P('ch', 'seq'), may hold values from -1.6 to 1.6
- skip_gain: float32 [4096], P('ch'), may hold values from -3 to 3
Outputs:
- mixed: bfloat16 [4096, 8192], P('ch', 'seq')
All inputs are finite; a program needn't handle non-finite values.
Results may differ from a plain program's by a relative error of at most 0.0075.
Values may be sent and summed in bfloat16 or wider, within the bound.
A program may use at most 192 MiB of HBM per device.

v0:
```python
import functools
import math

import jax
import jax.numpy as jnp
import numpy as np
from jax import lax
from jax.experimental import pallas as pl
from jax.experimental.pallas import tpu as pltpu
from jax.sharding import PartitionSpec as P

MIXER_CHANNELS = 4096
EPSILON = 1e-06
LANES = 128
GROUP = 16
BATCH = 4
VMEM_LIMIT = 56 * 1024 * 1024


def transform_tables(length):
    coarse = length // LANES
    k1 = np.arange(coarse)[:, None] + 0.25
    phi = 2.0 * np.pi * k1 * np.arange(coarse)[None, :] / coarse
    first = np.concatenate([np.cos(phi), -np.sin(phi)], axis=0)
    psi = 2.0 * np.pi * k1 * np.arange(LANES)[None, :] / length
    fine = np.arange(LANES)
    chi = 2.0 * np.pi * (fine[:, None] * fine[None, :] % LANES) / LANES
    c, s = np.cos(chi), np.sin(chi)
    second = np.block([[c, -s], [s, c]])
    second_inv = np.block([[c, s], [-s, c]])
    bf = jnp.bfloat16
    return (
        jnp.asarray(first, bf),
        jnp.asarray(first.T / length, bf),
        jnp.asarray(np.cos(psi), jnp.float32),
        jnp.asarray(np.sin(psi), jnp.float32),
        jnp.asarray(second, bf),
        jnp.asarray(second_inv, bf),
    )


def feature_kernel(group, taps, ids_ref, table_ref, taps_ref, first_ref, gated_ref, feats, carry):
    tokens = ids_ref.shape[-1]
    vocab = table_ref.shape[1]

    @pl.when(pl.program_id(0) == 0)
    def _():
        carry[...] = jnp.zeros_like(carry)

    ids = ids_ref[0]
    onehot = (lax.broadcasted_iota(jnp.int32, (vocab, tokens), 0) == ids).astype(jnp.bfloat16)
    feats[:, :LANES] = carry[...]
    feats[:, LANES:] = jnp.dot(table_ref[...], onehot, preferred_element_type=jnp.float32)
    carry[...] = feats[:, tokens:]
    rows = 8

    def stream(j, r):
        ext = feats[pl.ds(j * group + r, rows), :]
        weights = taps_ref[pl.ds(j * group + r, rows), :]
        acc = weights[:, 0:1] * ext[:, LANES:]
        for k in range(1, taps):
            acc = acc + weights[:, k : k + 1] * pltpu.roll(ext, k, 1)[:, LANES:]
        return acc

    @pl.loop(0, group // 16)
    def _(step):
        parts = []
        for half in range(2):
            r = pl.multiple_of(step * 16 + half * 8, 8)
            first_ref[0, pl.ds(r, rows), :] = stream(0, r)
            parts.append(stream(1, r) * stream(2, r))
        at = pl.multiple_of(step * 16, 16)
        gated_ref[0, pl.ds(at, 16), :] = jnp.concatenate(parts, axis=0).astype(jnp.bfloat16)


def conv_kernel(
    gated_ref, filter_ref, conv0_ref, skip_ref, t1_ref, t1i_ref, c_ref, s_ref, w2_ref, w2i_ref,
    out_ref, zs, hs, ys,
):
    blocks, group, tokens = gated_ref.shape
    per = tokens // LANES
    coarse = blocks * per
    f32, bf = jnp.float32, jnp.bfloat16

    for s in range(blocks):
        for q in range(per):
            cols = slice(q * LANES, (q + 1) * LANES)
            dst = pl.ds(s * per + q, group, stride=coarse)
            zs[dst, :] = gated_ref[s, :, cols].astype(f32)
            hs[dst, :] = filter_ref[s, :, cols].astype(f32)

    cos, sin = c_ref[...], s_ref[...]

    @pl.loop(0, group // BATCH)
    def _(step):
        base = pl.multiple_of(step * (BATCH * coarse), BATCH * coarse)
        parts = []
        for i in range(BATCH):
            at = pl.ds(base + i * coarse, coarse)
            both = jnp.concatenate([zs[at, :], hs[at, :]], axis=1).astype(bf)
            spread = jnp.dot(t1_ref[...], both, preferred_element_type=f32)
            for side in range(2):
                cols = slice(side * LANES, (side + 1) * LANES)
                re, im = spread[:coarse, cols], spread[coarse:, cols]
                parts.append(
                    jnp.concatenate([re * cos + im * sin, im * cos - re * sin], axis=1).astype(bf)
                )
        spectra = jnp.dot(jnp.concatenate(parts, axis=0), w2_ref[...], preferred_element_type=f32)
        parts = []
        for i in range(BATCH):
            z = spectra[2 * i * coarse : (2 * i + 1) * coarse]
            h = spectra[(2 * i + 1) * coarse : (2 * i + 2) * coarse]
            zr, zi, hr, hi = z[:, :LANES], z[:, LANES:], h[:, :LANES], h[:, LANES:]
            parts.append(jnp.concatenate([zr * hr - zi * hi, zr * hi + zi * hr], axis=1).astype(bf))
        back = jnp.dot(jnp.concatenate(parts, axis=0), w2i_ref[...], preferred_element_type=f32)
        for i in range(0, BATCH, 2):
            cols = []
            for o in range(2):
                p = back[(i + o) * coarse : (i + o + 1) * coarse]
                re, im = p[:, :LANES], p[:, LANES:]
                cols.append(jnp.concatenate([re * cos - im * sin, im * cos + re * sin], axis=0))
            res = jnp.dot(
                t1i_ref[...], jnp.concatenate(cols, axis=1).astype(bf), preferred_element_type=f32
            )
            for o in range(2):
                ys[pl.ds(base + (i + o) * coarse, coarse), :] = res[:, o * LANES : (o + 1) * LANES]

    skip = skip_ref[...]
    for s in range(blocks):
        for q in range(per):
            cols = slice(q * LANES, (q + 1) * LANES)
            conv = ys[pl.ds(s * per + q, group, stride=coarse), :]
            long_out = (conv + skip * gated_ref[s, :, cols].astype(f32)).astype(bf)
            out_ref[s, :, cols] = (conv0_ref[s, :, cols] * long_out.astype(f32)).astype(bf)


def features(ids, table, taps_rows, group, taps):
    blocks, _, tokens = ids.shape
    vocab = table.shape[1]
    return pl.pallas_call(
        functools.partial(feature_kernel, group, taps),
        grid=(blocks,),
        out_shape=(
            jax.ShapeDtypeStruct((blocks, group, tokens), jnp.float32),
            jax.ShapeDtypeStruct((blocks, group, tokens), jnp.bfloat16),
        ),
        in_specs=[
            pl.BlockSpec((1, 1, tokens), lambda i: (i, 0, 0)),
            pl.BlockSpec((3 * group, vocab), lambda i: (0, 0)),
            pl.BlockSpec((3 * group, taps), lambda i: (0, 0)),
        ],
        out_specs=(
            pl.BlockSpec((1, group, tokens), lambda i: (i, 0, 0)),
            pl.BlockSpec((1, group, tokens), lambda i: (i, 0, 0)),
        ),
        scratch_shapes=[
            pltpu.VMEM((3 * group, LANES + tokens), jnp.float32),
            pltpu.VMEM((3 * group, LANES), jnp.float32),
        ],
        compiler_params=pltpu.CompilerParams(vmem_limit_bytes=VMEM_LIMIT),
        cost_estimate=pl.CostEstimate(
            flops=2 * 3 * group * vocab * blocks * tokens,
            bytes_accessed=blocks * group * tokens * 6,
            transcendentals=0,
        ),
    )(ids, table, taps_rows)


def convolve(gated, filt, conv0, skip_rows):
    blocks, group, tokens = gated.shape
    length = blocks * tokens
    coarse = length // LANES
    tables = transform_tables(length)
    whole = lambda t: pl.BlockSpec(t.shape, lambda i: (0, 0))
    rows = pl.BlockSpec((blocks, GROUP, tokens), lambda i: (0, i, 0))
    return pl.pallas_call(
        conv_kernel,
        grid=(group // GROUP,),
        out_shape=jax.ShapeDtypeStruct((blocks, group, tokens), jnp.bfloat16),
        in_specs=[rows, rows, rows, pl.BlockSpec((GROUP, 1), lambda i: (i, 0))]
        + [whole(t) for t in tables],
        out_specs=rows,
        scratch_shapes=[pltpu.VMEM((GROUP * coarse, LANES), jnp.float32)] * 3,
        compiler_params=pltpu.CompilerParams(vmem_limit_bytes=VMEM_LIMIT),
        cost_estimate=pl.CostEstimate(
            flops=2 * group * coarse * 4 * 256 * 256,
            bytes_accessed=blocks * group * tokens * 10,
            transcendentals=0,
        ),
    )(gated, filt, conv0, skip_rows, *tables)


def shards(token_ids, embedding, projected, short_taps, long_filter, skip_gain):
    seq_count = lax.axis_size("seq")
    seq_index = lax.axis_index("seq")
    local_ch, vocab = embedding.shape
    tokens = token_ids.shape[0]
    taps = short_taps.shape[0]
    group = local_ch // seq_count
    start = seq_index * group

    filt = lax.all_to_all(
        long_filter.reshape(seq_count, group, tokens), "seq", split_axis=0, concat_axis=0, tiled=True
    )
    ids = lax.all_gather(token_ids.reshape(1, 1, tokens), "seq", axis=0, tiled=True)
    values = embedding.astype(jnp.float32)
    squares = lax.psum(jnp.sum(values * values, axis=0), "ch")
    vocab_scale = 1.0 / jnp.sqrt(squares / MIXER_CHANNELS + EPSILON)
    own = lax.dynamic_slice_in_dim(projected, start, group, axis=1)
    table = (own.astype(jnp.float32) * vocab_scale).astype(jnp.bfloat16)
    taps_rows = lax.dynamic_slice_in_dim(short_taps, start, group, axis=2).reshape(taps, 3 * group).T
    conv0, gated = features(ids, table.reshape(3 * group, vocab), taps_rows, group, taps)
    skip_rows = lax.dynamic_slice_in_dim(skip_gain, start, group)[:, None]
    mixed = convolve(gated, filt, conv0, skip_rows)
    returned = lax.all_to_all(mixed, "seq", split_axis=0, concat_axis=0, tiled=True)
    return returned.reshape(local_ch, tokens)


def solution(mesh):
    placed = (
        P("seq"),
        P("ch", None),
        P(None, "ch", None),
        P(None, None, "ch"),
        P("ch", "seq"),
        P("ch"),
    )
    return jax.shard_map(
        shards, mesh=mesh, in_specs=placed, out_specs=P("ch", "seq"), check_vma=False
    )
```

profile of v0, /device:TPU:0, one launch (start us, length us, event | category | flops | bytes accessed | tf_op | source)
XLA Modules:
  0.0 145.4 jit_solution(14797543474296072761)
XLA Ops:
  0.0 0.0 copy-start
  0.0 0.0 copy-start.2
  0.0 0.0 copy-start.3
  0.0 5.3 %all-to-all-start = ((bf16[8,128,1024]{2,1,0:T(8,128)(2,1)}), bf16[8,128,1024]{2,1,0:T(8,128)(2,1)S(1)}, u32[]{:S(2)}, u32[]{:S(2)}) async-start(bf16[8,128,1024]{2,1,0:T(8,128)(2,1)} %bitcast.10), calls=%async_computation | async-start | bytes 4194304 | tf_op jit(solution)/shard_map/all_to_all | solution.py:202
  5.3 0.8 dynamic-slice_bitcast_fusion
  6.1 0.7 copy.16.skip_ref
  6.8 0.0 copy-done
  6.8 0.8 copy.15
  7.7 0.0 copy-done.2
  7.7 0.3 multiply_reduce_fusion
  8.0 12.0 %psum.7 = f32[512]{0:T(512)S(1)} all-reduce(f32[512]{0:T(512)S(1)} %multiply_reduce_fusion), channel_id=1, replica_groups=mesh['seq'=8,'ch'=4] {'ch'}, use_global_device_ids=true, to_apply=%region_1.0 | all-reduce | flops 512 | bytes 4096 | tf_op jit(solution)/shard_map/psum | solution.py:207
  19.9 0.0 copy-done.3
  19.9 16.0 %all-gather = s32[8192]{0:T(1024)} all-gather(s32[1024]{0:T(1024)S(1)} %copy-done.3), channel_id=2, replica_groups=mesh['seq'=8,'ch'=4] {'seq'}, dimensions={0}, use_global_device_ids=true | all-gather | bytes 36864 | tf_op jit(solution)/shard_map/all_gather | solution.py:205
  36.0 1.8 %multiply_convert_fusion = bf16[3,128,512]{2,1,0:T(8,128)(2,1)} fusion(f32[512]{0:T(512)S(1)} %add_rsqrt_fusion, bf16[3,1024,512]{2,1,0:T(8,128)(2,1)} %param.14, s32[]{:T(128)S(6)} %select_n.2), kind=kLoop, calls=%fused_computation.1 | loop fusion | flops 589824 | bytes 788484 | tf_op jit(solution)/shard_map/convert_element_type | solution.py:210
  37.8 40.8 %shard_map.118 = (f32[8,128,1024]{2,1,0:T(8,128)}, bf16[8,128,1024]{2,1,0:T(8,128)(2,1)}) custom-call(s32[8,1,1024]{2,1,0:T(1,128)} %bitcast.13, bf16[384,512]{1,0:T(8,128)(2,1)} %bitcast.11, f32[384,7]{1,0:T(8,128)} %bitcast.12), custom_call_target="tpu_custom_call" | custom-call | flops 3221225472 | bytes 6291456 | tf_op jit(solution)/shard_map/pallas_call | solution.py:140
  78.6 0.0 all-to-all-done.filter_ref
  78.6 0.0 copy-start.1
  78.6 1.3 copy-done.1
  79.9 34.0 %shard_map.119 = bf16[8,128,1024]{2,1,0:T(8,128)(2,1)} custom-call(bf16[8,128,1024]{2,1,0:T(8,128)(2,1)} %get-tuple-element.7.gated_ref, bf16[8,128,1024]{2,1,0:T(8,128)(2,1)} %copy-done.1, f32[8,128,1024]{2,1,0:T(8,128)} %get-tuple-element.8.conv0_ref, f32[128,1]{1,0:T(8,128)} %copy.16.skip_ref, bf16[128,64]{1,0:T(8,128)(2,1)} %constant.32.clone.t1_ref, ...), custom_call_target="tpu_custom_call" | custom-call | flops 4294967296 | bytes 10485760 | tf_op jit(solution)/shard_map/pallas_call | solution.py:176
  114.0 30.1 %all_to_all.10 = bf16[8,128,1024]{2,1,0:T(8,128)(2,1)S(1)} all-to-all(bf16[8,128,1024]{2,1,0:T(8,128)(2,1)} %shard_map.119), channel_id=1, replica_groups=mesh['seq'=8,'ch'=4] {'seq'}, dimensions={0} | all-to-all | bytes 4194304 | tf_op jit(solution)/shard_map/all_to_all | solution.py:215
  144.1 1.3 copy.18
  (2 shorter events, 0.0 us)
Async XLA Ops:
  0.0 6.8 %copy-start = (f32[7,3,1024]{2,0,1:T(8,128)S(1)}, f32[7,3,1024]{2,0,1:T(8,128)}, u32[]{:S(2)}) copy-start(f32[7,3,1024]{2,0,1:T(8,128)} %param.15) | copy-start | bytes 258052
  0.0 7.7 %copy-start.2 = (bf16[1024,512]{1,0:T(8,128)(2,1)S(1)}, bf16[1024,512]{1,0:T(8,128)(2,1)}, u32[]{:S(2)}) copy-start(bf16[1024,512]{1,0:T(8,128)(2,1)} %param.13) | copy-start | bytes 3145732
  0.0 19.9 %copy-start.3 = (s32[1024]{0:T(1024)S(1)}, s32[1024]{0:T(1024)}, u32[]{:S(2)}) copy-start(s32[1024]{0:T(1024)} %param.12) | copy-start | bytes 12292
  0.0 78.6 %all-to-all-start = ((bf16[8,128,1024]{2,1,0:T(8,128)(2,1)}), bf16[8,128,1024]{2,1,0:T(8,128)(2,1)S(1)}, u32[]{:S(2)}, u32[]{:S(2)}) async-start(bf16[8,128,1024]{2,1,0:T(8,128)(2,1)} %bitcast.10), calls=%async_computation | async-start | bytes 4194304 | tf_op jit(solution)/shard_map/all_to_all | solution.py:202
  78.6 1.3 copy-start.1
where the time goes:
time: 146 us; the launch traced here: 145 us
  Pallas kernels  74.8 us (51%)
  blocking collectives  58.1 us (40%)
  starting transfers between devices  5.32 us (4%)
  local copies, waits for them, and re-layouts  5 us (3%)
  other arithmetic  2.09 us (1%)
    pallas_call x1, Pallas kernels, features(): pl.pallas_call(functools.partial(feature_kernel, group, taps), grid=(bloc...  40.8 us
    pallas_call x1, Pallas kernels, convolve(): pl.pallas_call(conv_kernel, grid=(group // GROUP,), out_shape=jax.ShapeDt...  34 us
    all_to_all x1, blocking collectives, shards(): lax.all_to_all(mixed, 'seq', split_axis=0, concat_axis=0, tiled=True)  30.1 us
    all_gather x1, blocking collectives, shards(): lax.all_gather(token_ids.reshape(1, 1, tokens), 'seq', axis=0, tiled=True)  16 us
    psum x1, blocking collectives, shards(): squares = lax.psum(jnp.sum(values * values, axis=0), 'ch')  12 us
    all_to_all x1, starting transfers between devices, shards(): lax.all_to_all(long_filter.reshape(seq_count, group, tokens), 'seq', spli...  5.32 us
  transfers between devices with their start and end apart: 1, of which 0 were waited for; matrix products, arithmetic and copies ran while one was open for 3% of the time, Pallas kernels for 28%

commit v1 on v0

--- a/solution.py
+++ b/solution.py
@@ -14,7 +14,9 @@
 LANES = 128
 GROUP = 16
 BATCH = 4
+HISTORY = 8
 VMEM_LIMIT = 56 * 1024 * 1024
+MESH = pl.DeviceIdType.MESH
 
 
 def transform_tables(length):
@@ -39,48 +41,123 @@
     )
 
 
-def feature_kernel(group, taps, ids_ref, table_ref, taps_ref, first_ref, gated_ref, feats, carry):
+def exchange_kernel(
+    seq_count, ch_count, ids_ref, squares_ref, ids_out, squares_out, send, recv, send_sq, recv_sq
+):
+    seq, ch = lax.axis_index("seq"), lax.axis_index("ch")
+    barrier = pltpu.get_barrier_semaphore()
+    for d in range(1, seq_count):
+        pl.semaphore_signal(
+            barrier, inc=1, device_id=(lax.rem(seq + d, seq_count), ch), device_id_type=MESH
+        )
+    for d in range(1, ch_count):
+        pl.semaphore_signal(
+            barrier, inc=1, device_id=(seq, lax.rem(ch + d, ch_count)), device_id_type=MESH
+        )
+    pl.semaphore_wait(barrier, seq_count + ch_count - 2)
+    copies = []
+    for d in range(1, ch_count):
+        copies.append(
+            pltpu.make_async_remote_copy(
+                src_ref=squares_ref,
+                dst_ref=squares_out.at[ch],
+                send_sem=send_sq.at[d],
+                recv_sem=recv_sq.at[d],
+                device_id=(seq, lax.rem(ch + d, ch_count)),
+                device_id_type=MESH,
+            )
+        )
+    for d in range(1, seq_count):
+        copies.append(
+            pltpu.make_async_remote_copy(
+                src_ref=ids_ref,
+                dst_ref=ids_out.at[seq],
+                send_sem=send.at[d],
+                recv_sem=recv.at[d],
+                device_id=(lax.rem(seq + d, seq_count), ch),
+                device_id_type=MESH,
+            )
+        )
+    for copy in copies:
+        copy.start()
+    ids_out[seq] = ids_ref[...]
+    squares_out[ch] = squares_ref[...]
+    for copy in copies:
+        copy.wait()
+
+
+def exchange(ids, squares, seq_count, ch_count):
+    vmem = pl.BlockSpec(memory_space=pltpu.VMEM)
+    dma = pltpu.SemaphoreType.DMA
+    return pl.pallas_call(
+        functools.partial(exchange_kernel, seq_count, ch_count),
+        out_shape=(
+            jax.ShapeDtypeStruct((seq_count,) + ids.shape, ids.dtype),
+            jax.ShapeDtypeStruct((ch_count,) + squares.shape, squares.dtype),
+        ),
+        in_specs=[vmem, vmem],
+        out_specs=(vmem, vmem),
+        scratch_shapes=[dma((seq_count,)), dma((seq_count,)), dma((ch_count,)), dma((ch_count,))],
+        compiler_params=pltpu.CompilerParams(collective_id=0, has_side_effects=True),
+    )(ids, squares)
+
+
+def feature_kernel(group, ids_ref, table_ref, taps_ref, first_ref, gated_ref, feats):
     tokens = ids_ref.shape[-1]
-    vocab = table_ref.shape[1]
+    vocab = table_ref.shape[0]
+    width = table_ref.shape[1] // 3
+    taps = taps_ref.shape[0]
 
     @pl.when(pl.program_id(0) == 0)
     def _():
-        carry[...] = jnp.zeros_like(carry)
-
-    ids = ids_ref[0]
-    onehot = (lax.broadcasted_iota(jnp.int32, (vocab, tokens), 0) == ids).astype(jnp.bfloat16)
-    feats[:, :LANES] = carry[...]
-    feats[:, LANES:] = jnp.dot(table_ref[...], onehot, preferred_element_type=jnp.float32)
-    carry[...] = feats[:, tokens:]
-    rows = 8
-
-    def stream(j, r):
-        ext = feats[pl.ds(j * group + r, rows), :]
-        weights = taps_ref[pl.ds(j * group + r, rows), :]
-        acc = weights[:, 0:1] * ext[:, LANES:]
+        feats[:HISTORY] = jnp.zeros((HISTORY, 3 * width), jnp.float32)
+
+    @pl.when(pl.program_id(0) > 0)
+    def _():
+        feats[:HISTORY] = feats[tokens:]
+
+    lane = lax.broadcasted_iota(jnp.int32, (LANES, vocab), 1)
+    for i in range(tokens // LANES):
+        ids = ids_ref[0, :, i * LANES : (i + 1) * LANES].astype(jnp.float32)
+        column = jnp.broadcast_to(ids, (LANES, LANES)).T.astype(jnp.int32)[:, :1]
+        onehot = (lane == column).astype(jnp.bfloat16)
+        feats[HISTORY + i * LANES : HISTORY + (i + 1) * LANES] = jnp.dot(
+            onehot, table_ref[...], preferred_element_type=jnp.float32
+        )
+
+    def stream(j, start):
+        cols = slice(j * width, (j + 1) * width)
+        acc = taps_ref[0:1, cols] * feats[start : start + LANES, cols]
         for k in range(1, taps):
-            acc = acc + weights[:, k : k + 1] * pltpu.roll(ext, k, 1)[:, LANES:]
+            acc = acc + taps_ref[k : k + 1, cols] * feats[start - k : start - k + LANES, cols]
         return acc
 
-    @pl.loop(0, group // 16)
-    def _(step):
-        parts = []
-        for half in range(2):
-            r = pl.multiple_of(step * 16 + half * 8, 8)
-            first_ref[0, pl.ds(r, rows), :] = stream(0, r)
-            parts.append(stream(1, r) * stream(2, r))
-        at = pl.multiple_of(step * 16, 16)
-        gated_ref[0, pl.ds(at, 16), :] = jnp.concatenate(parts, axis=0).astype(jnp.bfloat16)
+    for i in range(tokens // LANES):
+        cols = slice(i * LANES, (i + 1) * LANES)
+        start = HISTORY + i * LANES
+        gated_ref[0, :, cols] = (stream(1, start) * stream(2, start)).T[:group].astype(jnp.bfloat16)
+        first_ref[0, :, cols] = stream(0, start).T[:group]
 
 
 def conv_kernel(
     gated_ref, filter_ref, conv0_ref, skip_ref, t1_ref, t1i_ref, c_ref, s_ref, w2_ref, w2i_ref,
-    out_ref, zs, hs, ys,
+    out_ref, zs, hs, ys, send, send_sem, recv_sem, own_sem,
 ):
+    me, ch = lax.axis_index("seq"), lax.axis_index("ch")
+    step_at, steps = pl.program_id(0), pl.num_programs(0)
     blocks, group, tokens = gated_ref.shape
     per = tokens // LANES
     coarse = blocks * per
     f32, bf = jnp.float32, jnp.bfloat16
+
+    @pl.when(step_at == 0)
+    def _():
+        barrier = pltpu.get_barrier_semaphore()
+        for d in range(1, blocks):
+            pl.semaphore_signal(
+                barrier, inc=1, device_id=(lax.rem(me + d, blocks), ch), device_id_type=MESH
+            )
+        pl.semaphore_wait(barrier, blocks - 1)
 
     for s in range(blocks):
         for q in range(per):
@@ -131,14 +208,47 @@
             cols = slice(q * LANES, (q + 1) * LANES)
             conv = ys[pl.ds(s * per + q, group, stride=coarse), :]
             long_out = (conv + skip * gated_ref[s, :, cols].astype(f32)).astype(bf)
-            out_ref[s, :, cols] = (conv0_ref[s, :, cols] * long_out.astype(f32)).astype(bf)
-
-
-def features(ids, table, taps_rows, group, taps):
+            send[step_at, s, :, cols] = (conv0_ref[s, :, cols] * long_out.astype(f32)).astype(bf)
+
+    def rows_of(g):
+        return out_ref.at[me, pl.ds(pl.multiple_of(g * group, group), group), :]
+
+    def to_peer(g, d):
+        peer = lax.rem(me + d, blocks)
+        return pltpu.make_async_remote_copy(
+            src_ref=send.at[g, peer],
+            dst_ref=rows_of(g),
+            send_sem=send_sem.at[g, d],
+            recv_sem=recv_sem.at[g, d],
+            device_id=(peer, ch),
+            device_id_type=MESH,
+        )
+
+    def to_self(g):
+        return pltpu.make_async_copy(send.at[g, me], rows_of(g), own_sem.at[g])
+
+    @pl.loop(1, blocks)
+    def _(d):
+        to_peer(step_at, d).start()
+
+    to_self(step_at).start()
+
+    @pl.when(step_at == steps - 1)
+    def _():
+        @pl.loop(0, steps)
+        def _(g):
+            to_self(g).wait()
+
+            @pl.loop(1, blocks)
+            def _(d):
+                to_peer(g, d).wait()
+
+
+def features(ids, table, taps_rows, group):
     blocks, _, tokens = ids.shape
-    vocab = table.shape[1]
+    vocab, wide = table.shape
     return pl.pallas_call(
-        functools.partial(feature_kernel, group, taps),
+        functools.partial(feature_kernel, group),
         grid=(blocks,),
         out_shape=(
             jax.ShapeDtypeStruct((blocks, group, tokens), jnp.float32),
@@ -146,20 +256,17 @@
         ),
         in_specs=[
             pl.BlockSpec((1, 1, tokens), lambda i: (i, 0, 0)),
-            pl.BlockSpec((3 * group, vocab), lambda i: (0, 0)),
-            pl.BlockSpec((3 * group, taps), lambda i: (0, 0)),
+            pl.BlockSpec(table.shape, lambda i: (0, 0)),
+            pl.BlockSpec(taps_rows.shape, lambda i: (0, 0)),
         ],
         out_specs=(
             pl.BlockSpec((1, group, tokens), lambda i: (i, 0, 0)),
             pl.BlockSpec((1, group, tokens), lambda i: (i, 0, 0)),
         ),
-        scratch_shapes=[
-            pltpu.VMEM((3 * group, LANES + tokens), jnp.float32),
-            pltpu.VMEM((3 * group, LANES), jnp.float32),
-        ],
+        scratch_shapes=[pltpu.VMEM((HISTORY + tokens, wide), jnp.float32)],
         compiler_params=pltpu.CompilerParams(vmem_limit_bytes=VMEM_LIMIT),
         cost_estimate=pl.CostEstimate(
-            flops=2 * 3 * group * vocab * blocks * tokens,
+            flops=2 * wide * vocab * blocks * tokens,
             bytes_accessed=blocks * group * tokens * 6,
             transcendentals=0,
         ),
@@ -171,17 +278,27 @@
     length = blocks * tokens
     coarse = length // LANES
     tables = transform_tables(length)
+    groups = group // GROUP
+    dma = pltpu.SemaphoreType.DMA
     whole = lambda t: pl.BlockSpec(t.shape, lambda i: (0, 0))
     rows = pl.BlockSpec((blocks, GROUP, tokens), lambda i: (0, i, 0))
     return pl.pallas_call(
         conv_kernel,
-        grid=(group // GROUP,),
+        grid=(groups,),
         out_shape=jax.ShapeDtypeStruct((blocks, group, tokens), jnp.bfloat16),
         in_specs=[rows, rows, rows, pl.BlockSpec((GROUP, 1), lambda i: (i, 0))]
         + [whole(t) for t in tables],
-        out_specs=rows,
-        scratch_shapes=[pltpu.VMEM((GROUP * coarse, LANES), jnp.float32)] * 3,
-        compiler_params=pltpu.CompilerParams(vmem_limit_bytes=VMEM_LIMIT),
+        out_specs=pl.BlockSpec(memory_space=pl.ANY),
+        scratch_shapes=[pltpu.VMEM((GROUP * coarse, LANES), jnp.float32)] * 3
+        + [
+            pltpu.VMEM((groups, blocks, GROUP, tokens), jnp.bfloat16),
+            dma((groups, blocks)),
+            dma((groups, blocks)),
+            dma((groups,)),
+        ],
+        compiler_params=pltpu.CompilerParams(
+            vmem_limit_bytes=VMEM_LIMIT, collective_id=1, has_side_effects=True
+        ),
         cost_estimate=pl.CostEstimate(
             flops=2 * group * coarse * 4 * 256 * 256,
             bytes_accessed=blocks * group * tokens * 10,
@@ -199,21 +316,26 @@
     group = local_ch // seq_count
     start = seq_index * group
 
+    values = embedding.astype(jnp.float32)
+    squares = jnp.sum(values * values, axis=0)[None, :]
+    ids, squares = exchange(token_ids[None, :], squares, seq_count, lax.axis_size("ch"))
+    long_filter, ids = lax.optimization_barrier((long_filter, ids))
     filt = lax.all_to_all(
         long_filter.reshape(seq_count, group, tokens), "seq", split_axis=0, concat_axis=0, tiled=True
     )
-    ids = lax.all_gather(token_ids.reshape(1, 1, tokens), "seq", axis=0, tiled=True)
-    values = embedding.astype(jnp.float32)
-    squares = lax.psum(jnp.sum(values * values, axis=0), "ch")
-    vocab_scale = 1.0 / jnp.sqrt(squares / MIXER_CHANNELS + EPSILON)
+    vocab_scale = 1.0 / jnp.sqrt(jnp.sum(squares, axis=0) / MIXER_CHANNELS + EPSILON)
     own = lax.dynamic_slice_in_dim(projected, start, group, axis=1)
     table = (own.astype(jnp.float32) * vocab_scale).astype(jnp.bfloat16)
-    taps_rows = lax.dynamic_slice_in_dim(short_taps, start, group, axis=2).reshape(taps, 3 * group).T
-    conv0, gated = features(ids, table.reshape(3 * group, vocab), taps_rows, group, taps)
+    taps_rows = lax.dynamic_slice_in_dim(short_taps, start, group, axis=2)
+    width = -(-group // LANES) * LANES
+    if width != group:
+        table = jnp.pad(table, ((0, 0), (0, width - group), (0, 0)))
+        taps_rows = jnp.pad(taps_rows, ((0, 0), (0, 0), (0, width - group)))
+    conv0, gated = features(
+        ids, table.reshape(3 * width, vocab).T, taps_rows.reshape(taps, 3 * width), group
+    )
     skip_rows = lax.dynamic_slice_in_dim(skip_gain, start, group)[:, None]
-    mixed = convolve(gated, filt, conv0, skip_rows)
-    returned = lax.all_to_all(mixed, "seq", split_axis=0, concat_axis=0, tiled=True)
-    return returned.reshape(local_ch, tokens)
+    return convolve(gated, filt, conv0, skip_rows).reshape(local_ch, tokens)
 
 
 def solution(mesh):

time: 146 us -> 88.7 us (0.61)
  blocking collectives: 58.1 us -> 0 us
  Pallas kernels: 74.8 us -> 71.2 us
  waiting for transfers between devices: 0.01 us -> 2.7 us
  local copies, waits for them, and re-layouts: 5 us -> 7.43 us
  starting transfers between devices: 5.32 us -> 3.62 us
    all_to_all x1 -> x0, blocking collectives: 30.1 us -> none  [shards(): lax.all_to_all(mixed, 'seq', split_axis=0, concat_axis=0, tiled=True)]
    all_gather x1 -> x0, blocking collectives: 16 us -> none  [shards(): lax.all_gather(token_ids.reshape(1, 1, tokens), 'seq', axis=0, tiled=True)]
    psum x1 -> x0, blocking collectives: 12 us -> none  [shards(): squares = lax.psum(jnp.sum(values * values, axis=0), 'ch')]
    pallas_call x2 -> x3, Pallas kernels: 74.8 us -> 71.2 us  [the longest x1 40.9 us: convolve(): pl.pallas_call(conv_kernel, grid=(groups,), out_shape=jax.ShapeDtypeStruc...]
    all_to_all x1, waiting for transfers between devices: 0.01 us -> 2.7 us  [shards(): lax.all_to_all(long_filter.reshape(seq_count, group, tokens), 'seq', spli...]
    reduce_sum x1 -> x2, other arithmetic: 0.28 us -> 2.13 us  [the longest x1 2.11 us: shards(): squares = jnp.sum(values * values, axis=0)[None, :]]
    unnamed x9 -> x7, local copies, waits for them, and re-layouts: 2.65 us -> 4.41 us
    all_to_all x1, starting transfers between devices: 5.32 us -> 3.62 us  [shards(): lax.all_to_all(long_filter.reshape(seq_count, group, tokens), 'seq', spli...]
  transfers between devices with their start and end apart: 1 -> 1, of which waited for: 0 -> 1; matrix products, arithmetic and copies ran while one was open for 3% -> 5% of each run, Pallas kernels for 28% -> 22%
where the time goes in v1:
time: 88.7 us; the launch traced here: 88.3 us
  Pallas kernels  71.2 us (80%)
  local copies, waits for them, and re-layouts  7.43 us (8%)
  starting transfers between devices  3.62 us (4%)
  other arithmetic  3.22 us (4%)
  waiting for transfers between devices  2.7 us (3%)
    pallas_call x1, Pallas kernels, convolve(): pl.pallas_call(conv_kernel, grid=(groups,), out_shape=jax.ShapeDtypeStruc...  40.9 us
    pallas_call x1, Pallas kernels, features(): pl.pallas_call(functools.partial(feature_kernel, group), grid=(blocks,),...  19.7 us
    pallas_call x1, Pallas kernels, exchange(): pl.pallas_call(functools.partial(exchange_kernel, seq_count, ch_count), o...  10.6 us
    unnamed x7, local copies, waits for them, and re-layouts  4.41 us
    all_to_all x1, starting transfers between devices, shards(): lax.all_to_all(long_filter.reshape(seq_count, group, tokens), 'seq', spli...  3.62 us
    all_to_all x1, waiting for transfers between devices, shards(): lax.all_to_all(long_filter.reshape(seq_count, group, tokens), 'seq', spli...  2.7 us
    reduce_sum x1, other arithmetic, shards(): squares = jnp.sum(values * values, axis=0)[None, :]  2.11 us
  transfers between devices with their start and end apart: 1, of which 1 were waited for; matrix products, arithmetic and copies ran while one was open for 5% of the time, Pallas kernels for 22%

profile of v1, /device:TPU:0, one launch (start us, length us, event | category | flops | bytes accessed | tf_op | source)
XLA Modules:
  0.0 88.3 jit_solution(14205319077016399810)
XLA Ops:
  0.0 0.0 copy-start
  0.0 2.1 %multiply_reduce_fusion = f32[512]{0:T(512)} fusion(bf16[1024,512]{1,0:T(8,128)(2,1)} %param.13), kind=kLoop, calls=%fused_computation | loop fusion | flops 1572352 | bytes 1050624 | tf_op jit(solution)/shard_map/reduce_sum | solution.py:320
  2.1 10.6 %shard_map.118 = (s32[8,1,1024]{2,1,0:T(1,128)}, f32[4,1,512]{2,1,0:T(1,128)}) custom-call(s32[1,1024]{1,0:T(1,128)} %bitcast.15, f32[1,512]{1,0:T(1,128)} %bitcast.14), custom_call_target="tpu_custom_call" | custom-call | tf_op jit(solution)/shard_map/pallas_call | solution.py:92
  12.7 0.0 copy-start.2
  12.7 3.6 %all-to-all-start = ((bf16[8,128,1024]{2,1,0:T(8,128)(2,1)}), bf16[8,128,1024]{2,1,0:T(8,128)(2,1)S(1)}, u32[]{:S(2)}, u32[]{:S(2)}) async-start(bf16[8,128,1024]{2,1,0:T(8,128)(2,1)} %bitcast.10), calls=%async_computation | async-start | bytes 4194304 | tf_op jit(solution)/shard_map/all_to_all | solution.py:323
  16.4 0.8 dynamic-slice_bitcast_fusion.1
  17.1 0.7 copy.16.skip_ref
  17.9 0.0 copy-done.2
  17.9 1.1 %multiply_convert_fusion = bf16[3,128,512]{2,1,0:T(8,128)(2,1)S(1)} fusion(f32[512]{0:T(512)S(1)} %add_rsqrt_fusion, bf16[3,1024,512]{2,1,0:T(8,128)(2,1)} %param.14, s32[]{:T(128)S(6)} %select_n.2), kind=kLoop, calls=%fused_computation.1 | loop fusion | flops 589824 | bytes 788484 | tf_op jit(solution)/shard_map/convert_element_type | solution.py:328
  19.0 0.9 %copy.15 = bf16[384,512]{0,1:T(8,128)(2,1)} copy(bf16[384,512]{1,0:T(8,128)(2,1)S(1)} %bitcast.12) | data formatting | bytes 786432 | tf_op jit(solution)/shard_map/reshape | solution.py:335
  19.9 0.0 copy-done
  19.9 0.6 dynamic-slice_bitcast_fusion.taps_ref
  20.5 19.7 %shard_map.119 = (f32[8,128,1024]{2,1,0:T(8,128)}, bf16[8,128,1024]{2,1,0:T(8,128)(2,1)}) custom-call(s32[8,1,1024]{2,1,0:T(1,128)} %get-tuple-element.12.ids_ref, bf16[512,384]{1,0:T(8,128)(2,1)} %bitcast.13, f32[7,384]{1,0:T(8,128)} %dynamic-slice_bitcast_fusion.taps_ref), custom_call_target="tpu_custom_call" | custom-call | flops 3221225472 | bytes 6291456 | tf_op jit(solution)/shard_map/pallas_call | solution.py:250
  40.2 2.7 %all-to-all-done.filter_ref = bf16[8,128,1024]{2,1,0:T(8,128)(2,1)S(1)} async-done(((bf16[8,128,1024]{2,1,0:T(8,128)(2,1)}), bf16[8,128,1024]{2,1,0:T(8,128)(2,1)S(1)}, u32[]{:S(2)}, u32[]{:S(2)}) %all-to-all-start) | async-done | bytes 2097184 | tf_op jit(solution)/shard_map/all_to_all | solution.py:323
  42.9 0.0 copy-start.1
  42.9 1.3 %copy-done.1 = bf16[8,128,1024]{2,1,0:T(8,128)(2,1)} copy-done((bf16[8,128,1024]{2,1,0:T(8,128)(2,1)}, bf16[8,128,1024]{2,1,0:T(8,128)(2,1)S(1)}, u32[]{:S(2)}) %copy-start.1) | copy-done | bytes 2097176
  44.3 40.9 %shard_map.120 = bf16[8,128,1024]{2,1,0:T(8,128)(2,1)} custom-call(bf16[8,128,1024]{2,1,0:T(8,128)(2,1)} %get-tuple-element.14.gated_ref, bf16[8,128,1024]{2,1,0:T(8,128)(2,1)} %copy-done.1, f32[8,128,1024]{2,1,0:T(8,128)} %get-tuple-element.16.conv0_ref, f32[128,1]{1,0:T(8,128)} %copy.16.skip_ref, bf16[128,64]{1,0:T(8,128)(2,1)} %constant.32.clone.t1_ref, ...), custom_call_target="tpu_custom_call" | custom-call | flops 4294967296 | bytes 10485760 | tf_op jit(solution)/shard_map/pallas_call | solution.py:285
  85.2 3.1 %copy.18 = bf16[1024,1024]{1,0:T(8,128)(2,1)} copy(bf16[1024,1024]{1,0:T(8,128)(2,1)} %bitcast.11) | data formatting | bytes 4194304
  (2 shorter events, 0.0 us)
Async XLA Ops:
  0.0 19.9 %copy-start = (f32[7,3,1024]{2,0,1:T(8,128)S(1)}, f32[7,3,1024]{2,0,1:T(8,128)}, u32[]{:S(2)}) copy-start(f32[7,3,1024]{2,0,1:T(8,128)} %param.15) | copy-start | bytes 258052
  12.7 5.2 %copy-start.2 = (f32[4,1,512]{2,1,0:T(1,128)S(1)}, f32[4,1,512]{2,1,0:T(1,128)}, u32[]{:S(2)}) copy-start(f32[4,1,512]{2,1,0:T(1,128)} %get-tuple-element.13) | copy-start | bytes 24580
  12.7 30.2 %all-to-all-start = ((bf16[8,128,1024]{2,1,0:T(8,128)(2,1)}), bf16[8,128,1024]{2,1,0:T(8,128)(2,1)S(1)}, u32[]{:S(2)}, u32[]{:S(2)}) async-start(bf16[8,128,1024]{2,1,0:T(8,128)(2,1)} %bitcast.10), calls=%async_computation | async-start | bytes 4194304 | tf_op jit(solution)/shard_map/all_to_all | solution.py:323
  42.9 1.3 %copy-start.1 = (bf16[8,128,1024]{2,1,0:T(8,128)(2,1)}, bf16[8,128,1024]{2,1,0:T(8,128)(2,1)S(1)}, u32[]{:S(2)}) copy-start(bf16[8,128,1024]{2,1,0:T(8,128)(2,1)S(1)} %all-to-all-done.filter_ref) | copy-start | bytes 6291460
